TPU v7x, 256 devices: a whole 4x4x8 slice. The times are simulated.
256 devices in a mesh: lat: 8 (over z), lon: 32 (over x, y, core).
Axes of the slice: x: 4, y: 4, z: 8, core: 2. Of those that a mesh axis runs over, the one named last changes fastest.
Arguments:
- snapshots: bfloat16 [262144, 4096], P(('lat', 'lon')), may hold values from -24 to 24
- test_matrix: bfloat16 [4096, 256], replicated, may hold values from -0.09375 to 0.09375
Outputs:
- basis: float32 [262144, 256], P(('lat', 'lon'))
- projected: float32 [4096, 256], P('lon')
All inputs are finite; a program needn't handle non-finite values.
Results may differ from a plain program's by a relative error of at most 0.00037.
Values sent between devices are 32-bit elements; how exact they have to be, the bound alone decides.
A program may use at most 64 MiB of HBM per device.

v0:
```python
import jax
import jax.numpy as jnp
from jax import lax
from jax.sharding import PartitionSpec as P


def local(snapshots, test_matrix):
    sketch = jnp.dot(snapshots, test_matrix, preferred_element_type=jnp.float32)
    local_gram = jnp.dot(sketch.T, sketch, precision=lax.Precision.HIGHEST)
    gram = lax.psum(local_gram, ("lat", "lon"))
    lower = jnp.linalg.cholesky(gram)
    basis = jax.scipy.linalg.solve_triangular(lower, sketch.T, lower=True).T
    basis_b = basis.astype(jnp.bfloat16)
    snap_rows = snapshots.shape[1] // lax.axis_size("lon")
    term = lax.dot_general(
        snapshots, basis_b, (((0,), (0,)), ((), ())), preferred_element_type=jnp.float32
    )
    total = lax.psum(term, ("lat", "lon"))
    projected = lax.dynamic_slice_in_dim(total, lax.axis_index("lon") * snap_rows, snap_rows, 0)
    return (basis, projected)


def solution(mesh):
    return jax.shard_map(
        local,
        mesh=mesh,
        in_specs=(P(("lat", "lon"), None), P()),
        out_specs=(P(("lat", "lon"), None), P("lon", None)),
        check_vma=False,
    )
```

profile of v0, /device:TPU:32, one launch (start us, length us, event | category | flops | bytes accessed | tf_op | source)
XLA Modules:
  0.0 621.1 jit_solution(16401580001113740255)
XLA Ops:
  7.2 0.0 copy-start
  7.2 0.0 all-reduce.4.cloned.1.call-start
  7.2 1.5 copy-done
  8.8 5.7 fusion.10
  14.5 2.5 fusion.11
  17.0 0.0 all-reduce.4.cloned.1.call-update
  17.0 0.2 all-reduce.6.cloned.1.call-start
  17.3 250.6 %all-reduce.4.cloned.1.call-done = f32[256,256]{0,1:T(8,128)} async-done(((f32[256,256]{0,1:T(8,128)}), f32[256,256]{0,1:T(8,128)}) %all-reduce.4.cloned.1.call-update) | async-done | bytes 262160 | tf_op jit(solution)/shard_map/psum | solution.py:10
  267.9 1.1 copy.5
  269.0 1.0 fusion.3
  269.9 0.0 copy-start.4
  270.0 0.7 copy-done.4
  270.7 11.7 %cholesky.50 = f32[128,128]{1,0:T(8,128)S(1)} custom-call(f32[128,128]{1,0:T(8,128)S(1)} %cholesky.118), custom_call_target="Cholesky" | custom-call | tf_op jit(solution)/shard_map/jit(cholesky)/cholesky | solution.py:11
  282.4 9.8 %custom-call.15 = f32[1,128,128]{1,2,0:T(8,128)S(1)} custom-call(f32[1,128,128]{2,1,0:T(8,128)S(1)} %get-tuple-element.25), custom_call_target="InvertDiagBlocksLowerTriangular" | custom-call | tf_op jit(solution)/shard_map/jit(cholesky)/cholesky | solution.py:11
  292.2 1.0 constant_dynamic-update-slice_fusion
  293.3 1.1 convolution_subtract_fusion.1
  294.4 11.7 %cholesky.105 = f32[128,128]{1,0:T(8,128)S(1)} custom-call(f32[128,128]{1,0:T(8,128)S(1)} %convolution_subtract_fusion.1), custom_call_target="Cholesky" | custom-call | tf_op jit(solution)/shard_map/jit(cholesky)/cholesky | solution.py:11
  306.2 0.0 copy-start.3
  306.2 0.7 compare_reduce_fusion
  308.1 0.0 copy-done.3
  308.1 1.0 select_select_fusion
  309.1 0.1 triangular_solve.57
  309.2 5.5 while.1
  309.4 0.6 fusion.22
  310.0 2.1 bitcast_dynamic-update-slice_fusion.2
  312.1 0.6 fusion.22
  312.6 2.1 bitcast_dynamic-update-slice_fusion.2
  314.7 20.5 %custom-call.16 = f32[2,128,128]{1,2,0:T(8,128)S(1)} custom-call(f32[2,128,128]{2,1,0:T(8,128)} %get-tuple-element.9), custom_call_target="InvertDiagBlocksLowerTriangular" | custom-call | tf_op jit(solution)/shard_map/jit(_solve_triangular)/triangular_solve | solution.py:12
  335.2 0.6 fusion
  335.8 0.0 copy-start.1
  335.9 1.0 convolution_subtract_fusion
  336.9 0.6 fusion.5
  337.5 0.0 copy-done.1
  337.5 7.7 %convolution_bitcast_fusion = f32[4096,256]{0,1:T(8,128)} fusion(bf16[1024,4096]{1,0:T(8,128)(2,1)} %param.2, f32[128,1024]{1,0:T(8,128)S(1)} %fusion.5, f32[128,1024]{1,0:T(8,128)S(1)} %fusion), kind=kOutput, calls=%fused_computation.2 | convolution fusion | flops 2148532224 | bytes 13631488 | tf_op jit(solution)/shard_map/dot_general | solution.py:15
  345.2 0.0 copy-start.2
  345.2 0.0 all-reduce.6.cloned.1.call-update
  345.2 1.0 copy-done.2
  346.3 1.1 maximum_bitcast_fusion
  347.4 2.5 copy.6
  349.9 262.7 %all-reduce.6.cloned.1.call-done = f32[4096,256]{0,1:T(8,128)} async-done(((f32[4096,256]{0,1:T(8,128)}), f32[4096,256]{0,1:T(8,128)}) %all-reduce.6.cloned.1.call-update) | async-done | bytes 4194320 | tf_op jit(solution)/shard_map/psum | solution.py:18
  612.6 0.9 constant_dynamic-slice_fusion.1
  613.5 0.8 copy.7
  (8 shorter events, 0.1 us)
Async XLA Ops:
  7.2 1.6 copy-start
  7.2 260.7 %all-reduce.4.cloned.1.call-start = ((), (), s32[]{:S(2)}) async-start(), calls=%async_computation | async-start | bytes 524288 | tf_op jit(solution)/shard_map/psum | solution.py:10
  17.0 595.6 %all-reduce.6.cloned.1.call-start = ((), (), s32[]{:S(2)}) async-start(), calls=%async_computation.1 | async-start | bytes 8388608 | tf_op jit(solution)/shard_map/psum | solution.py:18
  269.9 0.7 copy-start.4
  306.2 2.0 copy-start.3
  335.8 1.7 copy-start.1
  345.2 1.0 copy-start.2
Sparse Core Ops, SparseCore 0:
  17.1 250.6 all-reduce.3
  345.4 267.2 all-reduce.5
where the time goes:
time: 624 us; the launch traced here: 621 us
  waiting for transfers between devices  513 us (82%)
  other arithmetic  57.6 us (9%)
  matrix products  20.4 us (3%)
  between operations  15.4 us (2%)
  local copies, waits for them, and re-layouts  14 us (2%)
    psum x1, waiting for transfers between devices, local(): total = lax.psum(term, ('lat', 'lon'))  263 us
    psum x1, waiting for transfers between devices, local(): gram = lax.psum(local_gram, ('lat', 'lon'))  251 us
    another operation x6, other arithmetic, local(): lower = jnp.linalg.cholesky(gram)  34 us
    another operation x3, other arithmetic, local(): basis = jax.scipy.linalg.solve_triangular(lower, sketch.T, lower=True).T  21.5 us
  transfers between devices with their start and end apart: 2, of which 2 were waited for; matrix products, arithmetic and copies ran while one was open for 1% of the time, Pallas kernels for 0%

commit v1 on v0

v1 whole, which is shorter than its diff:
```python
import functools

import jax
import jax.numpy as jnp
from jax import lax
from jax.experimental import pallas as pl
from jax.experimental.pallas import tpu as pltpu
from jax.sharding import PartitionSpec as P

MESH = pl.DeviceIdType.MESH
HIGHEST = lax.Precision.HIGHEST
f32, bf16 = jnp.float32, jnp.bfloat16
VMEM = pl.BlockSpec(memory_space=pltpu.VMEM)
ANY = pl.BlockSpec(memory_space=pl.ANY)

NX, NY, NZ = 4, 4, 8
ROWS, SNAPS, RANK = 1024, 4096, 256
PARTS = 4
PART = ROWS // PARTS
XY = [(dx, dy) for dx in range(NX) for dy in range(NY)]


def place():
    z, lon = lax.axis_index("lat"), lax.axis_index("lon")
    return lon // 8, (lon // 2) % 4, z, lon % 2


def device(x, y, z, c):
    return (z, (x * NY + y) * 2 + c)


def remote(src, dst, send, recv, where):
    return pltpu.make_async_remote_copy(
        src_ref=src, dst_ref=dst, send_sem=send, recv_sem=recv, device_id=where, device_id_type=MESH
    )


def tn(a, b, precision=None):
    return lax.dot_general(a, b, (((0,), (0,)), ((), ())), precision=precision, preferred_element_type=f32)


def nt(a, b, precision=None):
    return lax.dot_general(a, b, (((1,), (1,)), ((), ())), precision=precision, preferred_element_type=f32)


def greet(partners):
    barrier = pltpu.get_barrier_semaphore()
    for where in partners:
        pl.semaphore_signal(barrier, inc=1, device_id=where, device_id_type=MESH)


def gram_kernel(
    snap_ref, test_ref, sketch_ref, gram_ref,
    snap, test, half, from_core, from_xy, from_z, piece,
    load, cs, cr, xs, xr, zs, zr, gs, gr, hs, hr,
):
    x, y, z, c = place()
    core = device(x, y, z, 1 - c)
    xy = [device((x + dx) % NX, (y + dy) % NY, z, c) for dx, dy in XY[1:]]
    zz = [device(x, y, (z + dz) % NZ, c) for dz in range(1, NZ)]
    greet([core] + xy + zz)

    loads = [pltpu.make_async_copy(test_ref, test, load.at[PARTS])]
    for p in range(PARTS):
        rows = pl.ds(p * PART, PART)
        loads.append(pltpu.make_async_copy(snap_ref.at[rows], snap.at[rows], load.at[p]))
    for copy in loads:
        copy.start()
    loads[0].wait()
    cross = jnp.zeros((RANK, 2 * RANK), f32)
    low = jnp.zeros((RANK, RANK), f32)
    for p in range(PARTS):
        loads[p + 1].wait()
        rows = pl.ds(p * PART, PART)
        s = jnp.dot(snap[rows, :], test[...], preferred_element_type=f32)
        sketch_ref[rows, :] = s
        hi = s.astype(bf16)
        lo = (s - hi.astype(f32)).astype(bf16)
        cross += tn(hi, jnp.concatenate([hi, lo], axis=1))
        low += tn(lo, lo)
    mixed = cross[:, RANK:]
    gram = cross[:, :RANK] + (mixed + mixed.T + low)
    half[0] = gram[:128]
    half[1] = gram[128:]
    pl.semaphore_wait(pltpu.get_barrier_semaphore(), 1 + len(xy) + len(zz))

    copy = remote(half.at[1 - c], from_core, cs, cr, core)
    copy.start()
    copy.wait()
    from_core[...] += half[c]

    mine = x * NY + y
    copies = []
    for k, (dx, dy) in enumerate(XY[1:]):
        to = (x + dx) % NX * NY + (y + dy) % NY
        copy = remote(from_core.at[pl.ds(to * 8, 8)], from_xy.at[k], xs.at[k], xr.at[k], xy[k])
        copy.start()
        copies.append(copy)
    total = from_core[pl.ds(mine * 8, 8), :]
    for k, copy in enumerate(copies):
        copy.wait()
        total += from_xy[k]

    piece[...] = total
    from_z[z] = total
    copies = []
    for k in range(NZ - 1):
        copy = remote(piece, from_z.at[z], zs.at[k], zr.at[k], zz[k])
        copy.start()
        copies.append(copy)
    for copy in copies:
        copy.wait()
    total = from_z[0]
    for k in range(1, NZ):
        total += from_z[k]

    gram_ref[c, pl.ds(mine * 8, 8), :] = total
    copies = []
    for k in range(len(xy)):
        rows = gram_ref.at[c, pl.ds(mine * 8, 8)]
        copy = remote(rows, rows, gs.at[k], gr.at[k], xy[k])
        copy.start()
        copies.append(copy)
    for copy in copies:
        copy.wait()
    copy = remote(gram_ref.at[c], gram_ref.at[c], hs, hr, core)
    copy.start()
    copy.wait()


def factor_block(d, n=64):
    eye = (
        lax.broadcasted_iota(jnp.int32, (n, n), 0) == lax.broadcasted_iota(jnp.int32, (n, n), 1)
    ).astype(f32)
    both = jnp.concatenate([d, eye], axis=1)
    tiles = [both[8 * t : 8 * t + 8] for t in range(n // 8)]
    sub = lax.broadcasted_iota(jnp.int32, (8, 2 * n), 0)
    for k in range(n):
        first, s = divmod(k, 8)
        row = jnp.broadcast_to(tiles[first][s : s + 1, :], (8, 2 * n))
        pivot = jnp.broadcast_to(tiles[first][s : s + 1, k : k + 1], (8, 2 * n))
        scaled = row * (1.0 / pivot)
        for t in range(first, n // 8):
            if t == first and s == 7:
                continue
            column = jnp.broadcast_to(tiles[t][:, k : k + 1], (8, 2 * n))
            if t == first:
                column = jnp.where(sub > s, column, 0.0)
            tiles[t] = tiles[t] - column * scaled
    both = jnp.concatenate(tiles, axis=0)
    diagonal = jnp.sum(both[:, :n] * eye, axis=1, keepdims=True)
    return both[:, n:] * lax.rsqrt(diagonal)


def basis_kernel(gram_ref, sketch_ref, basis_ref, basis_b_ref, work, inverse):
    n = 64
    work[:, :RANK] = gram_ref[...]
    work[:, RANK:] = (
        lax.broadcasted_iota(jnp.int32, (RANK, RANK), 0)
        == lax.broadcasted_iota(jnp.int32, (RANK, RANK), 1)
    ).astype(f32)
    for b in range(RANK // n):
        lo, hi = b * n, (b + 1) * n
        r = jnp.dot(
            factor_block(work[lo:hi, lo:hi]), work[lo:hi, :], precision=HIGHEST, preferred_element_type=f32
        )
        inverse[lo:hi, :] = r[:, RANK:]
        if hi < RANK:
            work[hi:, :] = work[hi:, :] - tn(r[:, hi:RANK], r, HIGHEST)
    basis = nt(sketch_ref[...], inverse[...], HIGHEST)
    basis_ref[...] = basis
    basis_b_ref[...] = basis.astype(bf16)


def project_kernel(
    snap_ref, basis_ref, out_ref,
    snap, flipped, term, from_core, a1, b1, a2, b2, mine, from_z, piece, whole,
    load, cs, cr, a1s, a1r, b1s, b1r, a2s, a2r, b2s, b2r, zs, zr, gs, gr,
):
    x, y, z, c = place()
    core = device(x, y, z, 1 - c)
    xs = [device((x + d) % NX, y, z, c) for d in range(1, NX)]
    ys = [device(x, (y + d) % NY, z, c) for d in range(1, NY)]
    zz = [device(x, y, (z + d) % NZ, c) for d in range(1, NZ)]
    greet([core] + xs + ys + zz)
    for i in range(NX):
        columns = pl.ds((x + 1 + i) % NX * 1024, 1024)
        pltpu.make_async_copy(snap_ref.at[:, columns], snap.at[i], load.at[i]).start()
    flipped[...] = basis_ref[...].T
    pl.semaphore_wait(pltpu.get_barrier_semaphore(), 1 + len(xs) + len(ys) + len(zz))

    for i in range(NX):
        tx = (x + 1 + i) % NX
        pltpu.make_async_copy(snap_ref.at[:, pl.ds(tx * 1024, 1024)], snap.at[i], load.at[i]).wait()
        for j in range(NY):
            ty = (y + 1 + j) % NY
            r = jnp.dot(
                flipped[...], snap[i, :, pl.ds(pl.multiple_of(ty * 256, 256), 256)], preferred_element_type=f32
            )
            term[c, i, j] = r[:, :128]
            term[1 - c, i, j] = r[:, 128:]
            remote(term.at[1, i, j], from_core.at[i, j], cs.at[i, j], cr.at[i, j], core).start()

    first, second = pl.ds(0, 128), pl.ds(128, 128)
    for i in range(NX):
        for j in range(NY):
            copy = remote(term.at[1, i, j], from_core.at[i, j], cs.at[i, j], cr.at[i, j], core)
            copy.wait_recv()
            from_core[i, j] += term[0, i, j]
            if i < 3:
                remote(from_core.at[i, j, first], a1.at[i, j], a1s.at[i, j], a1r.at[i, j], xs[i]).start()
            if j < 3:
                remote(from_core.at[i, j, second], b1.at[j, i], b1s.at[j, i], b1r.at[j, i], ys[j]).start()

    def a_wait(j):
        for i in range(3):
            remote(from_core.at[i, j, first], a1.at[i, j], a1s.at[i, j], a1r.at[i, j], xs[i]).wait_recv()
        return from_core[3, j, :128] + (a1[0, j] + a1[1, j] + a1[2, j])

    def b_wait(i):
        for j in range(3):
            remote(from_core.at[i, j, second], b1.at[j, i], b1s.at[j, i], b1r.at[j, i], ys[j]).wait_recv()
        return from_core[i, 3, 128:] + (b1[0, i] + b1[1, i] + b1[2, i])

    late = []
    for k in range(3):
        a2[0, k] = a_wait(k)
        copy = remote(a2.at[0, k], a2.at[1, k], a2s.at[k], a2r.at[k], ys[k])
        copy.start()
        late.append(copy)
        b2[0, k] = b_wait(k)
        copy = remote(b2.at[0, k], b2.at[1, k], b2s.at[k], b2r.at[k], xs[k])
        copy.start()
        late.append(copy)
    mine[:128] = a_wait(3)
    mine[128:] = b_wait(3)
    for copy in late:
        copy.wait()
    mine[:128] += a2[1, 0] + a2[1, 1] + a2[1, 2]
    mine[128:] += b2[1, 0] + b2[1, 1] + b2[1, 2]

    copies = []
    for k in range(NZ - 1):
        copy = remote(mine.at[pl.ds((z + 1 + k) % NZ * 32, 32)], from_z.at[k], zs.at[k], zr.at[k], zz[k])
        copy.start()
        copies.append(copy)
    total = mine[pl.ds(z * 32, 32), :]
    for k, copy in enumerate(copies):
        copy.wait()
        total += from_z[k]
    piece[...] = total
    whole[pl.ds(z * 32, 32), :] = total
    copies = []
    for k in range(NZ - 1):
        copy = remote(piece, whole.at[pl.ds(z * 32, 32)], gs.at[k], gr.at[k], zz[k])
        copy.start()
        copies.append(copy)
    for copy in copies:
        copy.wait()
    out_ref[...] = whole[...].T

    for i in range(NX):
        for j in range(NY):
            remote(term.at[1, i, j], from_core.at[i, j], cs.at[i, j], cr.at[i, j], core).wait_send()
            if i < 3:
                remote(from_core.at[i, j, first], a1.at[i, j], a1s.at[i, j], a1r.at[i, j], xs[i]).wait_send()
            if j < 3:
                remote(from_core.at[i, j, second], b1.at[j, i], b1s.at[j, i], b1r.at[j, i], ys[j]).wait_send()


def sems(*shape):
    return pltpu.SemaphoreType.DMA(shape) if shape else pltpu.SemaphoreType.DMA


def local(snapshots, test_matrix):
    params = functools.partial(pltpu.CompilerParams, vmem_limit_bytes=56 * 2**20)
    sketch, gram = pl.pallas_call(
        gram_kernel,
        name="gram",
        out_shape=(
            jax.ShapeDtypeStruct((ROWS, RANK), f32),
            jax.ShapeDtypeStruct((2, RANK // 2, RANK), f32),
        ),
        in_specs=[ANY, ANY],
        out_specs=(VMEM, VMEM),
        scratch_shapes=[
            pltpu.VMEM((ROWS, SNAPS), bf16),
            pltpu.VMEM((SNAPS, RANK), bf16),
            pltpu.VMEM((2, 128, RANK), f32),
            pltpu.VMEM((128, RANK), f32),
            pltpu.VMEM((15, 8, RANK), f32),
            pltpu.VMEM((NZ, 8, RANK), f32),
            pltpu.VMEM((8, RANK), f32),
            sems(PARTS + 1),
            sems(), sems(), sems(15), sems(15), sems(7), sems(7), sems(15), sems(15), sems(), sems(),
        ],
        compiler_params=params(collective_id=0, has_side_effects=True),
    )(snapshots, test_matrix)
    basis, basis_b = pl.pallas_call(
        basis_kernel,
        name="basis",
        out_shape=(
            jax.ShapeDtypeStruct((ROWS, RANK), f32),
            jax.ShapeDtypeStruct((ROWS, RANK), bf16),
        ),
        in_specs=[VMEM, VMEM],
        out_specs=(VMEM, VMEM),
        scratch_shapes=[pltpu.VMEM((RANK, 2 * RANK), f32), pltpu.VMEM((RANK, RANK), f32)],
        compiler_params=params(),
    )(gram.reshape(RANK, RANK), sketch)
    projected = pl.pallas_call(
        project_kernel,
        name="project",
        out_shape=jax.ShapeDtypeStruct((128, RANK), f32),
        in_specs=[ANY, VMEM],
        out_specs=VMEM,
        scratch_shapes=[
            pltpu.VMEM((NX, ROWS, 1024), bf16),
            pltpu.VMEM((RANK, ROWS), bf16),
            pltpu.VMEM((2, NX, NY, RANK, 128), f32),
            pltpu.VMEM((NX, NY, RANK, 128), f32),
            pltpu.VMEM((3, NY, 128, 128), f32),
            pltpu.VMEM((3, NX, 128, 128), f32),
            pltpu.VMEM((2, 3, 128, 128), f32),
            pltpu.VMEM((2, 3, 128, 128), f32),
            pltpu.VMEM((RANK, 128), f32),
            pltpu.VMEM((7, 32, 128), f32),
            pltpu.VMEM((32, 128), f32),
            pltpu.VMEM((RANK, 128), f32),
            sems(NX),
            sems(NX, NY), sems(NX, NY),
            sems(3, NY), sems(3, NY), sems(3, NX), sems(3, NX),
            sems(3), sems(3), sems(3), sems(3),
            sems(7), sems(7), sems(7), sems(7),
        ],
        compiler_params=params(collective_id=1, has_side_effects=True),
    )(snapshots, basis_b)
    return basis, projected


def solution(mesh):
    return jax.shard_map(
        local,
        mesh=mesh,
        in_specs=(P(("lat", "lon"), None), P()),
        out_specs=(P(("lat", "lon"), None), P("lon", None)),
        check_vma=False,
    )
```

time: 624 us -> 115 us (0.18)
  waiting for transfers between devices: 513 us -> 0 us
  Pallas kernels: 0 us -> 113 us
  other arithmetic: 57.6 us -> 0 us
  matrix products: 20.4 us -> 0 us
  between operations: 15.4 us -> 0.65 us
  local copies, waits for them, and re-layouts: 14 us -> 1.57 us
    psum x2 -> x0, waiting for transfers between devices: 513 us -> none  [the longest x1 263 us: local(): total = lax.psum(term, ('lat', 'lon'))]
    pallas_call x0 -> x3, Pallas kernels: none -> 113 us  [the longest x1 41 us: local(): pl.pallas_call(project_kernel, name='project', out_shape=jax.ShapeDtypeSt...]
    another operation x9 -> x0, other arithmetic: 55.5 us -> none  [the longest x6 34 us: local(): lower = jnp.linalg.cholesky(gram)]
    dot_general x3 -> x0, matrix products: 15.9 us -> none  [the longest x1 7.69 us: local(): lax.dot_general(snapshots, basis_b, (((0,), (0,)), ((), ())), preferred_e...]
  transfers between devices with their start and end apart: 2 -> 0, of which waited for: 2 -> 0; matrix products, arithmetic and copies ran while one was open for 1% -> 0% of each run, Pallas kernels for 0% -> 0%
where the time goes in v1:
time: 115 us
  Pallas kernels  113 us (98%)
  local copies, waits for them, and re-layouts  1.57 us (1%)
    pallas_call x1, Pallas kernels, local(): pl.pallas_call(project_kernel, name='project', out_shape=jax.ShapeDtypeSt...  41 us
    pallas_call x1, Pallas kernels, local(): pl.pallas_call(basis_kernel, name='basis', out_shape=(jax.ShapeDtypeStruc...  39.4 us
    pallas_call x1, Pallas kernels, local(): pl.pallas_call(gram_kernel, name='gram', out_shape=(jax.ShapeDtypeStruct(...  32.4 us

profile of v1, /device:TPU:32, one launch (start us, length us, event | category | flops | bytes accessed | tf_op | source)
XLA Modules:
  0.0 115.0 jit_solution(16360302994919299213)
XLA Ops:
  0.6 32.4 %gram.1 = (f32[1024,256]{1,0:T(8,128)}, f32[2,128,256]{2,1,0:T(8,128)}) custom-call(bf16[1024,4096]{1,0:T(8,128)(2,1)} %snap_ref.3, bf16[4096,256]{1,0:T(8,128)(2,1)} %test_ref.1), custom_call_target="tpu_custom_call" | custom-call | tf_op jit(solution)/shard_map/gram/pallas_call | solution.py:277
  33.1 39.4 %basis.1 = (f32[1024,256]{1,0:T(8,128)}, bf16[1024,256]{1,0:T(8,128)(2,1)}) custom-call(f32[256,256]{1,0:T(8,128)} %bitcast.1, f32[1024,256]{1,0:T(8,128)} %get-tuple-element.7.sketch_ref), custom_call_target="tpu_custom_call" | custom-call | tf_op jit(solution)/shard_map/basis/pallas_call | solution.py:299
  72.4 41.0 %project.1 = f32[128,256]{1,0:T(8,128)} custom-call(bf16[1024,4096]{1,0:T(8,128)(2,1)} %snap_ref.3, bf16[1024,256]{1,0:T(8,128)(2,1)} %get-tuple-element.9.basis_ref), custom_call_target="tpu_custom_call" | custom-call | tf_op jit(solution)/shard_map/project/pallas_call | solution.py:311
  113.5 1.6 %copy.5 = f32[128,256]{1,0:T(8,128)} copy(f32[128,256]{1,0:T(8,128)} %project.1) | data formatting | bytes 262144

commit v2 on v0

v2 whole, which is shorter than its diff:
```python
import functools

import jax
import jax.numpy as jnp
from jax import lax
from jax.experimental import pallas as pl
from jax.experimental.pallas import tpu as pltpu
from jax.sharding import PartitionSpec as P

MESH = pl.DeviceIdType.MESH
HIGHEST = lax.Precision.HIGHEST
f32, bf16 = jnp.float32, jnp.bfloat16
VMEM = pl.BlockSpec(memory_space=pltpu.VMEM)
ANY = pl.BlockSpec(memory_space=pl.ANY)

NX, NY, NZ = 4, 4, 8
ROWS, SNAPS, RANK = 1024, 4096, 256
PARTS = 4
PART = ROWS // PARTS
XY = [(dx, dy) for dx in range(NX) for dy in range(NY)]
ORDER = sorted(XY, key=lambda ij: (max(ij), ij))
RA, RB, RC = 96, 96, 64
RAB = RA + RB


def place():
    z, lon = lax.axis_index("lat"), lax.axis_index("lon")
    return lon // 8, (lon // 2) % 4, z, lon % 2


def device(x, y, z, c):
    return (z, (x * NY + y) * 2 + c)


def remote(src, dst, send, recv, where):
    return pltpu.make_async_remote_copy(
        src_ref=src, dst_ref=dst, send_sem=send, recv_sem=recv, device_id=where, device_id_type=MESH
    )


def tn(a, b, precision=None):
    return lax.dot_general(a, b, (((0,), (0,)), ((), ())), precision=precision, preferred_element_type=f32)


def nt(a, b, precision=None):
    return lax.dot_general(a, b, (((1,), (1,)), ((), ())), precision=precision, preferred_element_type=f32)


def greet(partners):
    barrier = pltpu.get_barrier_semaphore()
    for where in partners:
        pl.semaphore_signal(barrier, inc=1, device_id=where, device_id_type=MESH)


def lanes(v, j):
    return jnp.broadcast_to(v[:, j : j + 1], (8, 128))


def row(v, s):
    return jnp.broadcast_to(v[s : s + 1, :], (8, 128))


def factor_block(d, n=64):
    eye = (
        lax.broadcasted_iota(jnp.int32, (n, n), 0) == lax.broadcasted_iota(jnp.int32, (n, n), 1)
    ).astype(f32)
    both = jnp.concatenate([d, eye], axis=1)
    count = n // 8
    tiles = [both[8 * t : 8 * t + 8] for t in range(count)]
    sub = lax.broadcasted_iota(jnp.int32, (8, 128), 0)
    ahead = [lanes(tiles[0], j) for j in range(8)]
    for p in range(count):
        base = 8 * p
        cols = {p: ahead}
        if p + 1 < count:
            ahead = [lanes(tiles[p + 1], base + 8 + j) for j in range(8)]
        for t in range(p + 1, count):
            cols[t] = [lanes(tiles[t], base + j) for j in range(8)]
        for k in range(8):
            inv = 1.0 / row(cols[p][k], k)
            m = {t: cols[t][k] * inv for t in range(p, count)}
            for j in range(k + 1, 8):
                b = row(cols[p][k], j)
                cols[p][j] = cols[p][j] - (cols[p][k] * b) * inv
                for t in range(p + 1, count):
                    cols[t][j] = cols[t][j] - m[t] * b
            if p + 1 < count:
                for j in range(8):
                    ahead[j] = ahead[j] - m[p + 1] * row(cols[p + 1][k], j)
            pivot_row = row(tiles[p], k)
            if k < 7:
                tiles[p] = tiles[p] - jnp.where(sub > k, m[p], 0.0) * pivot_row
            for t in range(p + 1, count):
                tiles[t] = tiles[t] - m[t] * pivot_row
    both = jnp.concatenate(tiles, axis=0)
    diagonal = jnp.sum(both[:, :n] * eye, axis=1, keepdims=True)
    return both[:, n:] * lax.rsqrt(diagonal)


def kernel(
    snap_ref, test_ref, basis_ref, out_ref,
    snap, test, sketch, basis,
    half, from_core, from_xy, from_z, piece, gram, work, inverse,
    flipped, term, sums, a1, b1, c1, a2, b2, c2, csum, mine, z1, part, whole,
    load, store, gcs, gcr, gxs, gxr, gzs, gzr, gbs, gbr, ghs, ghr,
    cs, cr, a1s, a1r, b1s, b1r, c1s, c1r, a2s, a2r, b2s, b2r, c2s, c2r, zs, zr, ws, wr,
):
    x, y, z, c = place()
    core = device(x, y, z, 1 - c)
    xy = [device((x + dx) % NX, (y + dy) % NY, z, c) for dx, dy in XY[1:]]
    xs = [device((x + d) % NX, y, z, c) for d in range(1, NX)]
    ys = [device(x, (y + d) % NY, z, c) for d in range(1, NY)]
    zz = [device(x, y, (z + dz) % NZ, c) for dz in range(1, NZ)]
    greet([core] + xy + zz)

    loads = [pltpu.make_async_copy(test_ref, test, load.at[PARTS])]
    for p in range(PARTS):
        rows = pl.ds(p * PART, PART)
        loads.append(pltpu.make_async_copy(snap_ref.at[rows], snap.at[rows], load.at[p]))
    for copy in loads:
        copy.start()
    loads[0].wait()
    cross = jnp.zeros((RANK, 2 * RANK), f32)
    low = jnp.zeros((RANK, RANK), f32)
    for p in range(PARTS):
        loads[p + 1].wait()
        rows = pl.ds(p * PART, PART)
        s = jnp.dot(snap[rows, :], test[...], preferred_element_type=f32)
        sketch[rows, :] = s
        hi = s.astype(bf16)
        lo = (s - hi.astype(f32)).astype(bf16)
        cross += tn(hi, jnp.concatenate([hi, lo], axis=1))
        low += tn(lo, lo)
    mixed = cross[:, RANK:]
    term_gram = cross[:, :RANK] + (mixed + mixed.T + low)
    half[0] = term_gram[:128]
    half[1] = term_gram[128:]
    pl.semaphore_wait(pltpu.get_barrier_semaphore(), 1 + len(xy) + len(zz))

    copy = remote(half.at[1 - c], from_core, gcs, gcr, core)
    copy.start()
    copy.wait()
    from_core[...] += half[c]
    own = x * NY + y
    copies = []
    for k, (dx, dy) in enumerate(XY[1:]):
        to = (x + dx) % NX * NY + (y + dy) % NY
        copy = remote(from_core.at[pl.ds(to * 8, 8)], from_xy.at[k], gxs.at[k], gxr.at[k], xy[k])
        copy.start()
        copies.append(copy)
    total = from_core[pl.ds(own * 8, 8), :]
    for k, copy in enumerate(copies):
        copy.wait()
        total += from_xy[k]
    piece[...] = total
    from_z[z] = total
    copies = []
    for k in range(NZ - 1):
        copy = remote(piece, from_z.at[z], gzs.at[k], gzr.at[k], zz[k])
        copy.start()
        copies.append(copy)
    for copy in copies:
        copy.wait()
    total = from_z[0]
    for k in range(1, NZ):
        total += from_z[k]
    gram[c, pl.ds(own * 8, 8), :] = total
    copies = []
    for k in range(len(xy)):
        rows = gram.at[c, pl.ds(own * 8, 8)]
        copy = remote(rows, rows, gbs.at[k], gbr.at[k], xy[k])
        copy.start()
        copies.append(copy)
    for copy in copies:
        copy.wait()
    copy = remote(gram.at[c], gram.at[c], ghs, ghr, core)
    copy.start()
    copy.wait()

    n = 64
    work[:128, :RANK] = gram[0]
    work[128:, :RANK] = gram[1]
    work[:, RANK:] = (
        lax.broadcasted_iota(jnp.int32, (RANK, RANK), 0)
        == lax.broadcasted_iota(jnp.int32, (RANK, RANK), 1)
    ).astype(f32)
    for b in range(RANK // n):
        lo, hi = b * n, (b + 1) * n
        inv = factor_block(work[lo:hi, lo:hi])
        r = jnp.dot(inv, work[lo:hi, :], precision=HIGHEST, preferred_element_type=f32)
        inverse[lo:hi, :] = r[:, RANK:]
        if hi < RANK:
            below = nt(work[hi:, lo:hi], inv, HIGHEST)
            work[hi:, :] = work[hi:, :] - jnp.dot(below, r, precision=HIGHEST, preferred_element_type=f32)

    for p in range(PARTS):
        rows = pl.ds(p * PART, PART)
        s = nt(sketch[rows, :], inverse[...], HIGHEST)
        basis[rows, :] = s
        flipped[:, p * PART : (p + 1) * PART] = s.astype(bf16).T
    out_copy = pltpu.make_async_copy(basis, basis_ref, store)
    out_copy.start()

    to_core, to_x, to_y, to_z = [], [], [], []
    lag = 4
    for step in range(len(ORDER) + lag):
        if step < len(ORDER):
            i, j = ORDER[step]
            chip = (x + 1 + i) % NX * NY + (y + 1 + j) % NY
            r = jnp.dot(
                flipped[...], snap[:, pl.ds(pl.multiple_of(chip * 256, 256), 256)], preferred_element_type=f32
            )
            term[c, step] = r[:, :128]
            term[1 - c, step] = r[:, 128:]
            copy = remote(term.at[1, step], sums.at[step], cs.at[step], cr.at[step], core)
            copy.start()
            to_core.append(copy)
        if step >= lag:
            m = step - lag
            i, j = ORDER[m]
            to_core[m].wait_recv()
            sums[m] += term[0, m]
            if i < 3:
                copy = remote(sums.at[m, pl.ds(0, RA)], a1.at[i, j], a1s.at[i, j], a1r.at[i, j], xs[i])
                copy.start()
                to_x.append(copy)
            if j < 3:
                copy = remote(sums.at[m, pl.ds(RA, RB)], b1.at[j, i], b1s.at[j, i], b1r.at[j, i], ys[j])
                copy.start()
                to_y.append(copy)
            if m % 4 == 3:
                g = m // 4
                for k in range(NZ - 1):
                    rows = pl.ds(pl.multiple_of(RAB + (z + 1 + k) % NZ * 8, 8), 8)
                    copy = remote(
                        sums.at[pl.ds(4 * g, 4), rows], c1.at[k, pl.ds(4 * g, 4)], c1s.at[k, g], c1r.at[k, g], zz[k]
                    )
                    copy.start()
                    to_z.append(copy)

    at = {ij: m for m, ij in enumerate(ORDER)}

    def a_sum(j):
        for i in range(3):
            remote(a1.at[i, j], a1.at[i, j], a1s.at[i, j], a1r.at[i, j], xs[i]).wait_recv()
        return sums[at[3, j], :RA] + (a1[0, j] + a1[1, j] + a1[2, j])

    def b_sum(i):
        for j in range(3):
            remote(b1.at[j, i], b1.at[j, i], b1s.at[j, i], b1r.at[j, i], ys[j]).wait_recv()
        return sums[at[i, 3], RA:RAB] + (b1[0, i] + b1[1, i] + b1[2, i])

    late = []
    for k in range(3):
        a2[0, k] = a_sum(k)
        copy = remote(a2.at[0, k], a2.at[1, k], a2s.at[k], a2r.at[k], ys[k])
        copy.start()
        late.append(copy)
        b2[0, k] = b_sum(k)
        copy = remote(b2.at[0, k], b2.at[1, k], b2s.at[k], b2r.at[k], xs[k])
        copy.start()
        late.append(copy)
    mine[:RA] = a_sum(3)
    mine[RA:] = b_sum(3)

    for copy in to_z:
        copy.wait_recv()
    own_rows = pl.ds(pl.multiple_of(RAB + z * 8, 8), 8)
    total = sums[:, own_rows, :]
    for k in range(NZ - 1):
        total += c1[k]
    csum[...] = total
    to_xy = []
    for k, (dx, dy) in enumerate(XY[1:]):
        m = at[(dx - 1) % 4, (dy - 1) % 4]
        copy = remote(csum.at[m], c2.at[k], c2s.at[k], c2r.at[k], xy[k])
        copy.start()
        to_xy.append(copy)

    for copy in late:
        copy.wait()
    mine[:RA] += a2[1, 0] + a2[1, 1] + a2[1, 2]
    mine[RA:] += b2[1, 0] + b2[1, 1] + b2[1, 2]
    share = RAB // NZ
    copies = []
    for k in range(NZ - 1):
        rows = pl.ds(pl.multiple_of((z + 1 + k) % NZ * share, 8), share)
        copy = remote(mine.at[rows], z1.at[k], zs.at[k], zr.at[k], zz[k])
        copy.start()
        copies.append(copy)
    total = csum[at[3, 3]]
    for k, copy in enumerate(to_xy):
        copy.wait()
        total += c2[k]
    part[share:] = total
    total = mine[pl.ds(pl.multiple_of(z * share, 8), share), :]
    for k, copy in enumerate(copies):
        copy.wait()
        total += z1[k]
    part[:share] = total

    whole[z] = part[...]
    copies = []
    for k in range(NZ - 1):
        copy = remote(part, whole.at[z], ws.at[k], wr.at[k], zz[k])
        copy.start()
        copies.append(copy)
    for copy in copies:
        copy.wait()
    for k in range(NZ):
        out_ref[:, share * k : share * (k + 1)] = whole[k, :share].T
        out_ref[:, RAB + 8 * k : RAB + 8 * (k + 1)] = whole[k, share:].T

    for copy in to_core + to_x + to_y + to_z:
        copy.wait_send()
    out_copy.wait()


def sems(*shape):
    return pltpu.SemaphoreType.DMA(shape) if shape else pltpu.SemaphoreType.DMA


def local(snapshots, test_matrix):
    return pl.pallas_call(
        kernel,
        name="range_finder",
        out_shape=(
            jax.ShapeDtypeStruct((ROWS, RANK), f32),
            jax.ShapeDtypeStruct((128, RANK), f32),
        ),
        in_specs=[ANY, ANY],
        out_specs=(ANY, VMEM),
        scratch_shapes=[
            pltpu.VMEM((ROWS, SNAPS), bf16),
            pltpu.VMEM((SNAPS, RANK), bf16),
            pltpu.VMEM((ROWS, RANK), f32),
            pltpu.VMEM((ROWS, RANK), f32),
            pltpu.VMEM((2, 128, RANK), f32),
            pltpu.VMEM((128, RANK), f32),
            pltpu.VMEM((15, 8, RANK), f32),
            pltpu.VMEM((NZ, 8, RANK), f32),
            pltpu.VMEM((8, RANK), f32),
            pltpu.VMEM((2, 128, RANK), f32),
            pltpu.VMEM((RANK, 2 * RANK), f32),
            pltpu.VMEM((RANK, RANK), f32),
            pltpu.VMEM((RANK, ROWS), bf16),
            pltpu.VMEM((2, 16, RANK, 128), f32),
            pltpu.VMEM((16, RANK, 128), f32),
            pltpu.VMEM((3, NY, RA, 128), f32),
            pltpu.VMEM((3, NX, RB, 128), f32),
            pltpu.VMEM((7, 16, 8, 128), f32),
            pltpu.VMEM((2, 3, RA, 128), f32),
            pltpu.VMEM((2, 3, RB, 128), f32),
            pltpu.VMEM((15, 8, 128), f32),
            pltpu.VMEM((16, 8, 128), f32),
            pltpu.VMEM((RAB, 128), f32),
            pltpu.VMEM((7, RAB // NZ, 128), f32),
            pltpu.VMEM((32, 128), f32),
            pltpu.VMEM((NZ, 32, 128), f32),
            sems(PARTS + 1), sems(),
            sems(), sems(), sems(15), sems(15), sems(7), sems(7), sems(15), sems(15), sems(), sems(),
            sems(16), sems(16),
            sems(3, NY), sems(3, NY), sems(3, NX), sems(3, NX), sems(7, 4), sems(7, 4),
            sems(3), sems(3), sems(3), sems(3), sems(15), sems(15),
            sems(7), sems(7), sems(7), sems(7),
        ],
        compiler_params=pltpu.CompilerParams(
            collective_id=0, has_side_effects=True, vmem_limit_bytes=56 * 2**20
        ),
    )(snapshots, test_matrix)


def solution(mesh):
    return jax.shard_map(
        local,
        mesh=mesh,
        in_specs=(P(("lat", "lon"), None), P()),
        out_specs=(P(("lat", "lon"), None), P("lon", None)),
        check_vma=False,
    )
```

time: 624 us -> 78 us (0.12)
  waiting for transfers between devices: 513 us -> 0 us
  Pallas kernels: 0 us -> 72.5 us
  other arithmetic: 57.6 us -> 0 us
  matrix products: 20.4 us -> 0 us
  between operations: 15.4 us -> 0.64 us
  local copies, waits for them, and re-layouts: 14 us -> 3.83 us
    psum x2 -> x0, waiting for transfers between devices: 513 us -> none  [the longest x1 263 us: local(): total = lax.psum(term, ('lat', 'lon'))]
    pallas_call x0 -> x1, Pallas kernels: none -> 72.5 us  [local(): pl.pallas_call(kernel, name='range_finder', out_shape=(jax.ShapeDtypeStru...]
    another operation x9 -> x0, other arithmetic: 55.5 us -> none  [the longest x6 34 us: local(): lower = jnp.linalg.cholesky(gram)]
    dot_general x3 -> x0, matrix products: 15.9 us -> none  [the longest x1 7.69 us: local(): lax.dot_general(snapshots, basis_b, (((0,), (0,)), ((), ())), preferred_e...]
  transfers between devices with their start and end apart: 2 -> 0, of which waited for: 2 -> 0; matrix products, arithmetic and copies ran while one was open for 1% -> 0% of each run, Pallas kernels for 0% -> 0%
where the time goes in v2:
time: 78 us; the launch traced here: 77 us
  Pallas kernels  72.5 us (93%)
  local copies, waits for them, and re-layouts  3.83 us (5%)
    pallas_call x1, Pallas kernels, local(): pl.pallas_call(kernel, name='range_finder', out_shape=(jax.ShapeDtypeStru...  72.5 us
    unnamed x2, local copies, waits for them, and re-layouts  3.83 us

profile of v2, /device:TPU:32, one launch (start us, length us, event | category | flops | bytes accessed | tf_op | source)
XLA Modules:
  0.0 77.0 jit_solution(4039834824096189355)
XLA Ops:
  0.6 72.5 %range_finder.1 = (f32[1024,256]{1,0:T(8,128)}, f32[128,256]{1,0:T(8,128)}) custom-call(bf16[1024,4096]{1,0:T(8,128)(2,1)} %snap_ref.1, bf16[4096,256]{1,0:T(8,128)(2,1)} %test_ref.1), custom_call_target="tpu_custom_call" | custom-call | tf_op jit(solution)/shard_map/range_finder/pallas_call | solution.py:324
  73.2 2.3 %copy.6 = f32[1024,256]{1,0:T(8,128)} copy(f32[1024,256]{1,0:T(8,128)} %get-tuple-element.4) | data formatting | bytes 2097152
  75.4 1.6 %copy.7 = f32[128,256]{1,0:T(8,128)} copy(f32[128,256]{1,0:T(8,128)} %get-tuple-element.5) | data formatting | bytes 262144

commit v3 on v2

v3 whole, which is shorter than its diff:
```python
import functools

import jax
import jax.numpy as jnp
from jax import lax
from jax.experimental import pallas as pl
from jax.experimental.pallas import tpu as pltpu
from jax.sharding import PartitionSpec as P

MESH = pl.DeviceIdType.MESH
HIGHEST = lax.Precision.HIGHEST
f32, bf16 = jnp.float32, jnp.bfloat16
VMEM = pl.BlockSpec(memory_space=pltpu.VMEM)
ANY = pl.BlockSpec(memory_space=pl.ANY)

NX, NY, NZ = 4, 4, 8
ROWS, SNAPS, RANK = 1024, 4096, 256
PARTS = 4
PART = ROWS // PARTS
RA, RB, RC = 96, 96, 64
RAB = RA + RB


def place():
    z, lon = lax.axis_index("lat"), lax.axis_index("lon")
    return lax.div(lon, 8), lax.rem(lax.div(lon, 2), 4), z, lax.rem(lon, 2)


def device(x, y, z, c):
    return (z, (x * NY + y) * 2 + c)


def remote(src, dst, send, recv, where):
    return pltpu.make_async_remote_copy(
        src_ref=src, dst_ref=dst, send_sem=send, recv_sem=recv, device_id=where, device_id_type=MESH
    )


def tn(a, b, precision=None):
    return lax.dot_general(a, b, (((0,), (0,)), ((), ())), precision=precision, preferred_element_type=f32)


def nt(a, b, precision=None):
    return lax.dot_general(a, b, (((1,), (1,)), ((), ())), precision=precision, preferred_element_type=f32)


def lanes(v, j):
    return jnp.broadcast_to(v[:, j : j + 1], (8, 128))


def row(v, s):
    return jnp.broadcast_to(v[s : s + 1, :], (8, 128))


def factor_block(d, n=64):
    eye = (
        lax.broadcasted_iota(jnp.int32, (n, n), 0) == lax.broadcasted_iota(jnp.int32, (n, n), 1)
    ).astype(f32)
    both = jnp.concatenate([d, eye], axis=1)
    count = n // 8
    tiles = [both[8 * t : 8 * t + 8] for t in range(count)]
    sub = lax.broadcasted_iota(jnp.int32, (8, 128), 0)
    ahead = [lanes(tiles[0], j) for j in range(8)]
    for p in range(count):
        base = 8 * p
        cols = {p: ahead}
        if p + 1 < count:
            ahead = [lanes(tiles[p + 1], base + 8 + j) for j in range(8)]
        for t in range(p + 1, count):
            cols[t] = [lanes(tiles[t], base + j) for j in range(8)]
        for k in range(8):
            inv = 1.0 / row(cols[p][k], k)
            m = {t: cols[t][k] * inv for t in range(p, count)}
            for j in range(k + 1, 8):
                b = row(cols[p][k], j)
                cols[p][j] = cols[p][j] - (cols[p][k] * b) * inv
                for t in range(p + 1, count):
                    cols[t][j] = cols[t][j] - m[t] * b
            if p + 1 < count:
                for j in range(8):
                    ahead[j] = ahead[j] - m[p + 1] * row(cols[p + 1][k], j)
            pivot_row = row(tiles[p], k)
            if k < 7:
                tiles[p] = tiles[p] - jnp.where(sub > k, m[p], 0.0) * pivot_row
            for t in range(p + 1, count):
                tiles[t] = tiles[t] - m[t] * pivot_row
    both = jnp.concatenate(tiles, axis=0)
    diagonal = jnp.sum(both[:, :n] * eye, axis=1, keepdims=True)
    return both[:, n:] * lax.rsqrt(diagonal)


def kernel(
    snap_ref, test_ref, basis_ref, out_ref,
    snap, test, sketch, basis,
    half, from_core, from_xy, from_z, piece, gram, work, inverse,
    flipped, term, sums, a1, b1, c1, a2, b2, c2, csum, mine, z1,
    load, store, gcs, gcr, gxs, gxr, gzs, gzr, gbs, gbr, ghs, ghr,
    cs, cr, a1s, a1r, b1s, b1r, c1s, c1r, a2s, a2r, b2s, b2r, c2s, c2r, zs, zr, ws, wr,
):
    x, y, z, c = place()
    core = device(x, y, z, 1 - c)

    def along_x(d):
        return device(lax.rem(x + d, NX), y, z, c)

    def along_y(d):
        return device(x, lax.rem(y + d, NY), z, c)

    def along_z(d):
        return device(x, y, lax.rem(z + d, NZ), c)

    def on_plane(k):
        return device(lax.rem(x + lax.div(k, NY), NX), lax.rem(y + lax.rem(k, NY), NY), z, c)

    def loop(first, last, body):
        lax.fori_loop(first, last, lambda k, _: (body(k), 0)[1], 0)

    def part(p):
        rows = pl.ds(pl.multiple_of(p * PART, PART), PART)
        return rows, pltpu.make_async_copy(snap_ref.at[rows], snap.at[rows], load.at[p])

    whole_test = pltpu.make_async_copy(test_ref, test, load.at[PARTS])
    whole_test.start()
    loop(0, PARTS, lambda p: part(p)[1].start())
    barrier = pltpu.get_barrier_semaphore()

    def greet(where):
        pl.semaphore_signal(barrier, inc=1, device_id=where, device_id_type=MESH)

    greet(core)
    loop(1, NX * NY, lambda k: greet(on_plane(k)))
    loop(1, NZ, lambda k: greet(along_z(k)))
    whole_test.wait()

    def sketch_part(p):
        rows, copy = part(p)
        copy.wait()
        sketch[rows, :] = jnp.dot(snap[rows, :], test[...], preferred_element_type=f32)

    loop(0, PARTS, sketch_part)
    hi = sketch[...].astype(bf16)
    lo = (sketch[...] - hi.astype(f32)).astype(bf16)
    cross = tn(hi, jnp.concatenate([hi, lo], axis=1))
    low = tn(lo, lo)
    mixed = cross[:, RANK:]
    term_gram = cross[:, :RANK] + (mixed + mixed.T + low)
    half[0] = term_gram[:128]
    half[1] = term_gram[128:]
    pl.semaphore_wait(barrier, 1 + (NX * NY - 1) + (NZ - 1))

    copy = remote(half.at[1 - c], from_core, gcs, gcr, core)
    copy.start()
    copy.wait()
    from_core[...] += half[c]

    def rows_of(cx, cy):
        return pl.ds(pl.multiple_of((cx * NY + cy) * 8, 8), 8)

    def scatter(k):
        rows = rows_of(lax.rem(x + lax.div(k, NY), NX), lax.rem(y + lax.rem(k, NY), NY))
        remote(from_core.at[rows], from_xy.at[k - 1], gxs, gxr, on_plane(k)).start()

    own = rows_of(x, y)
    loop(1, NX * NY, scatter)
    remote(from_xy, from_xy, gxs, gxr, core).wait()
    total = from_core[own, :]
    for k in range(NX * NY - 1):
        total += from_xy[k]
    piece[...] = total
    loop(1, NZ, lambda k: remote(piece, from_z.at[z], gzs, gzr, along_z(k)).start())
    from_z[z] = total
    remote(from_z.at[pl.ds(0, NZ - 1)], from_z.at[pl.ds(0, NZ - 1)], gzs, gzr, core).wait()
    total = from_z[0]
    for k in range(1, NZ):
        total += from_z[k]
    gram[c, own, :] = total
    mine_of_gram = gram.at[c, own]

    def back(k):
        return remote(mine_of_gram, mine_of_gram, gbs, gbr.at[k - 1], on_plane(k))

    loop(1, NX * NY, lambda k: back(k).start())
    loop(1, NX * NY, lambda k: back(k).wait_recv())
    copy = remote(gram.at[c], gram.at[c], ghs, ghr, core)
    copy.start()
    copy.wait()
    remote(from_xy, from_xy, gbs, gxr, core).wait_send()

    n = 64
    work[:128, :RANK] = gram[0]
    work[128:, :RANK] = gram[1]
    work[:, RANK:] = (
        lax.broadcasted_iota(jnp.int32, (RANK, RANK), 0)
        == lax.broadcasted_iota(jnp.int32, (RANK, RANK), 1)
    ).astype(f32)
    for b in range(RANK // n):
        lo, hi = b * n, (b + 1) * n
        inv = factor_block(work[lo:hi, lo:hi])
        r = jnp.dot(inv, work[lo:hi, :], precision=HIGHEST, preferred_element_type=f32)
        inverse[lo:hi, :] = r[:, RANK:]
        if hi < RANK:
            below = nt(work[hi:, lo:hi], inv, HIGHEST)
            work[hi:, :] = work[hi:, :] - jnp.dot(below, r, precision=HIGHEST, preferred_element_type=f32)

    for p in range(PARTS):
        rows = pl.ds(p * PART, PART)
        s = nt(sketch[rows, :], inverse[...], HIGHEST)
        basis[rows, :] = s
        flipped[:, p * PART : (p + 1) * PART] = s.astype(bf16).T
    out_copy = pltpu.make_async_copy(basis, basis_ref, store)
    out_copy.start()

    to_a, to_b = pl.ds(0, RA), pl.ds(RA, RB)
    blocks = NX * NY
    lag = 4

    def to_core(m):
        return remote(term.at[1, m], sums.at[m], cs, cr.at[m], core)

    def step(n):
        @pl.when(n < blocks)
        def _():
            cx, cy = lax.rem(x + 1 + lax.div(n, NY), NX), lax.rem(y + 1 + lax.rem(n, NY), NY)
            columns = pl.ds(pl.multiple_of((cx * NY + cy) * 256, 256), 256)
            r = jnp.dot(flipped[...], snap[:, columns], preferred_element_type=f32)
            term[c, n] = r[:, :128]
            term[1 - c, n] = r[:, 128:]
            to_core(n).start()

        @pl.when(n >= lag)
        def _():
            m = n - lag
            i, j = lax.div(m, NY), lax.rem(m, NY)
            to_core(m).wait_recv()
            sums[m] += term[0, m]

            @pl.when(i < NX - 1)
            def _():
                remote(sums.at[m, to_a], a1.at[j, i], a1s, a1r.at[j], along_x(i + 1)).start()

            @pl.when(j < NY - 1)
            def _():
                remote(sums.at[m, to_b], b1.at[i, j], b1s, b1r.at[i], along_y(j + 1)).start()

            @pl.when(j == NY - 1)
            def _():
                group = pl.ds(pl.multiple_of(i * NY, NY), NY)

                def to_z(k):
                    rows = pl.ds(pl.multiple_of(RAB + lax.rem(z + k, NZ) * 8, 8), 8)
                    remote(sums.at[group, rows], c1.at[k - 1, group], c1s, c1r, along_z(k)).start()

                loop(1, NZ, to_z)

    loop(0, blocks + lag, step)

    def a_sum(j):
        remote(a1.at[j], a1.at[j], a1s, a1r.at[j], core).wait_recv()
        return sums[(NX - 1) * NY + j, :RA] + (a1[j, 0] + a1[j, 1] + a1[j, 2])

    def b_sum(i):
        remote(b1.at[i], b1.at[i], b1s, b1r.at[i], core).wait_recv()
        return sums[i * NY + NY - 1, RA:RAB] + (b1[i, 0] + b1[i, 1] + b1[i, 2])

    for k in range(3):
        b2[0, k] = b_sum(k)
        remote(b2.at[0, k], b2.at[1, k], b2s, b2r, along_x(k + 1)).start()
    for k in range(3):
        a2[0, k] = a_sum(k)
        remote(a2.at[0, k], a2.at[1, k], a2s, a2r, along_y(k + 1)).start()
    mine[RA:] = b_sum(3)
    mine[:RA] = a_sum(3)
    remote(a2.at[0], a2.at[1], a2s, a2r, core).wait_recv()
    remote(b2.at[0], b2.at[1], b2s, b2r, core).wait_recv()
    mine[:RA] += a2[1, 0] + a2[1, 1] + a2[1, 2]
    mine[RA:] += b2[1, 0] + b2[1, 1] + b2[1, 2]
    share = RAB // NZ

    def to_z1(k):
        rows = pl.ds(pl.multiple_of(lax.rem(z + k, NZ) * share, 8), share)
        remote(mine.at[rows], z1.at[k - 1], zs, zr, along_z(k)).start()

    loop(1, NZ, to_z1)

    remote(c1, c1, c1s, c1r, core).wait_recv()
    own_rows = pl.ds(pl.multiple_of(RAB + z * 8, 8), 8)
    total = sums[:, own_rows, :]
    for k in range(NZ - 1):
        total += c1[k]
    csum[...] = total

    def to_plane(k):
        i = lax.rem(lax.div(k, NY) + NX - 1, NX)
        j = lax.rem(lax.rem(k, NY) + NY - 1, NY)
        remote(csum.at[i * NY + j], c2.at[k - 1], c2s, c2r, on_plane(k)).start()

    loop(1, blocks, to_plane)

    def gather(rows, which):
        def one(k):
            return remote(out_ref.at[rows], out_ref.at[rows], ws.at[which], wr.at[which, k - 1], along_z(k))

        return one

    rows = pl.ds(pl.multiple_of(z * share, 8), share)
    total = mine[rows, :]
    remote(z1, z1, zs, zr, core).wait()
    for k in range(NZ - 1):
        total += z1[k]
    out_ref[rows, :] = total
    large = gather(rows, 0)
    loop(1, NZ, lambda k: large(k).start())
    total = csum[blocks - 1]
    remote(c2, c2, c2s, c2r, core).wait()
    for k in range(blocks - 1):
        total += c2[k]
    out_ref[own_rows, :] = total
    small = gather(own_rows, 1)
    loop(1, NZ, lambda k: small(k).start())
    remote(z1, z1, ws.at[0], zr, core).wait_send()
    remote(c2.at[pl.ds(0, NZ - 1)], c2.at[pl.ds(0, NZ - 1)], ws.at[1], zr, core).wait_send()
    remote(term.at[1], sums, cs, zr, core).wait_send()
    remote(a1, a1, a1s, zr, core).wait_send()
    remote(b1, b1, b1s, zr, core).wait_send()
    remote(c1, c1, c1s, zr, core).wait_send()
    remote(a2.at[0], a2.at[1], a2s, zr, core).wait_send()
    remote(b2.at[0], b2.at[1], b2s, zr, core).wait_send()
    out_copy.wait()
    loop(1, NZ, lambda k: large(k).wait_recv())
    loop(1, NZ, lambda k: small(k).wait_recv())


def sems(*shape):
    return pltpu.SemaphoreType.DMA(shape) if shape else pltpu.SemaphoreType.DMA


def finish(basis_in, flat, basis_ref, out_ref):
    basis_ref[...] = basis_in[...]
    out_ref[...] = flat[...].T


def local(snapshots, test_matrix):
    basis, flat = pl.pallas_call(
        kernel,
        name="range_finder",
        out_shape=(
            jax.ShapeDtypeStruct((ROWS, RANK), f32),
            jax.ShapeDtypeStruct((RANK, 128), f32),
        ),
        in_specs=[ANY, ANY],
        out_specs=(ANY, VMEM),
        scratch_shapes=[
            pltpu.VMEM((ROWS, SNAPS), bf16),
            pltpu.VMEM((SNAPS, RANK), bf16),
            pltpu.VMEM((ROWS, RANK), f32),
            pltpu.VMEM((ROWS, RANK), f32),
            pltpu.VMEM((2, 128, RANK), f32),
            pltpu.VMEM((128, RANK), f32),
            pltpu.VMEM((15, 8, RANK), f32),
            pltpu.VMEM((NZ, 8, RANK), f32),
            pltpu.VMEM((8, RANK), f32),
            pltpu.VMEM((2, 128, RANK), f32),
            pltpu.VMEM((RANK, 2 * RANK), f32),
            pltpu.VMEM((RANK, RANK), f32),
            pltpu.VMEM((RANK, ROWS), bf16),
            pltpu.VMEM((2, 16, RANK, 128), f32),
            pltpu.VMEM((16, RANK, 128), f32),
            pltpu.VMEM((NY, 3, RA, 128), f32),
            pltpu.VMEM((NX, 3, RB, 128), f32),
            pltpu.VMEM((7, 16, 8, 128), f32),
            pltpu.VMEM((2, 3, RA, 128), f32),
            pltpu.VMEM((2, 3, RB, 128), f32),
            pltpu.VMEM((15, 8, 128), f32),
            pltpu.VMEM((16, 8, 128), f32),
            pltpu.VMEM((RAB, 128), f32),
            pltpu.VMEM((7, RAB // NZ, 128), f32),
            sems(PARTS + 1), sems(),
            sems(), sems(), sems(), sems(), sems(), sems(), sems(), sems(15), sems(), sems(),
            sems(), sems(16),
            sems(), sems(NY), sems(), sems(NX), sems(), sems(),
            sems(), sems(), sems(), sems(), sems(), sems(),
            sems(), sems(), sems(2), sems(2, 7),
        ],
        compiler_params=pltpu.CompilerParams(
            collective_id=0, has_side_effects=True, vmem_limit_bytes=56 * 2**20
        ),
    )(snapshots, test_matrix)
    return pl.pallas_call(
        finish,
        name="finish",
        out_shape=(
            jax.ShapeDtypeStruct((ROWS, RANK), f32),
            jax.ShapeDtypeStruct((128, RANK), f32),
        ),
        in_specs=[VMEM, VMEM],
        out_specs=(VMEM, VMEM),
    )(basis, flat)


def solution(mesh):
    return jax.shard_map(
        local,
        mesh=mesh,
        in_specs=(P(("lat", "lon"), None), P()),
        out_specs=(P(("lat", "lon"), None), P("lon", None)),
        check_vma=False,
    )
```

time: 78 us -> 70.5 us (0.904)
  local copies, waits for them, and re-layouts: 3.83 us -> 0 us
  Pallas kernels: 72.5 us -> 68.8 us
    pallas_call x1, Pallas kernels: 72.5 us -> 66.5 us  [local(): pl.pallas_call(kernel, name='range_finder', out_shape=(jax.ShapeDtypeStru...]
    unnamed x2 -> x0, local copies, waits for them, and re-layouts: 3.83 us -> none
    pallas_call x0 -> x1, Pallas kernels: none -> 2.31 us  [local(): pl.pallas_call(finish, name='finish', out_shape=(jax.ShapeDtypeStruct((RO...]
where the time goes in v3:
time: 70.5 us; the launch traced here: 69.4 us
  Pallas kernels  68.8 us (98%)
    pallas_call x1, Pallas kernels, local(): pl.pallas_call(kernel, name='range_finder', out_shape=(jax.ShapeDtypeStru...  66.5 us
    pallas_call x1, Pallas kernels, local(): pl.pallas_call(finish, name='finish', out_shape=(jax.ShapeDtypeStruct((RO...  2.31 us

profile of v3, /device:TPU:32, one launch (start us, length us, event | category | flops | bytes accessed | tf_op | source)
XLA Modules:
  0.0 69.4 jit_solution(3865694734254500777)
XLA Ops:
  0.6 66.5 %range_finder.1 = (f32[1024,256]{1,0:T(8,128)}, f32[256,128]{1,0:T(8,128)}) custom-call(bf16[1024,4096]{1,0:T(8,128)(2,1)} %snap_ref.1, bf16[4096,256]{1,0:T(8,128)(2,1)} %test_ref.1), custom_call_target="tpu_custom_call" | custom-call | tf_op jit(solution)/shard_map/range_finder/pallas_call | solution.py:343
  67.1 2.3 %finish.1 = (f32[1024,256]{1,0:T(8,128)}, f32[128,256]{1,0:T(8,128)}) custom-call(f32[1024,256]{1,0:T(8,128)} %get-tuple-element.4.basis_in, f32[256,128]{1,0:T(8,128)} %get-tuple-element.5.flat), custom_call_target="tpu_custom_call" | custom-call | tf_op jit(solution)/shard_map/finish/pallas_call | solution.py:388

commit v4 on v3

--- a/solution.py
+++ b/solution.py
@@ -91,7 +91,7 @@
 
 def kernel(
     snap_ref, test_ref, basis_ref, out_ref,
-    snap, test, sketch, basis,
+    snap, test, sketch, split, basis,
     half, from_core, from_xy, from_z, piece, gram, work, inverse,
     flipped, term, sums, a1, b1, c1, a2, b2, c2, csum, mine, z1,
     load, store, gcs, gcr, gxs, gxr, gzs, gzr, gbs, gbr, ghs, ghr,
@@ -115,6 +115,12 @@
     def loop(first, last, body):
         lax.fori_loop(first, last, lambda k, _: (body(k), 0)[1], 0)
 
+    def plane(body):
+        loop(0, NX * NY - 1, lambda t: body(1 + lax.rem(25 - t, NX * NY - 1)))
+
+    def ring(body):
+        loop(0, NZ - 1, lambda t: body(1 + lax.rem(11 - t, NZ - 1)))
+
     def part(p):
         rows = pl.ds(pl.multiple_of(p * PART, PART), PART)
         return rows, pltpu.make_async_copy(snap_ref.at[rows], snap.at[rows], load.at[p])
@@ -128,8 +134,8 @@
         pl.semaphore_signal(barrier, inc=1, device_id=where, device_id_type=MESH)
 
     greet(core)
-    loop(1, NX * NY, lambda k: greet(on_plane(k)))
-    loop(1, NZ, lambda k: greet(along_z(k)))
+    plane(lambda k: greet(on_plane(k)))
+    ring(lambda k: greet(along_z(k)))
     whole_test.wait()
 
     def sketch_part(p):
@@ -139,19 +145,29 @@
 
     loop(0, PARTS, sketch_part)
     hi = sketch[...].astype(bf16)
-    lo = (sketch[...] - hi.astype(f32)).astype(bf16)
-    cross = tn(hi, jnp.concatenate([hi, lo], axis=1))
-    low = tn(lo, lo)
-    mixed = cross[:, RANK:]
-    term_gram = cross[:, :RANK] + (mixed + mixed.T + low)
-    half[0] = term_gram[:128]
-    half[1] = term_gram[128:]
-    pl.semaphore_wait(barrier, 1 + (NX * NY - 1) + (NZ - 1))
-
-    copy = remote(half.at[1 - c], from_core, gcs, gcr, core)
-    copy.start()
-    copy.wait()
-    from_core[...] += half[c]
+    split[0] = hi
+    split[1] = (sketch[...] - hi.astype(f32)).astype(bf16)
+
+    def gram_half(h):
+        columns = pl.ds(pl.multiple_of(h * 128, 128), 128)
+        left = jnp.concatenate([split[0, :, columns], split[1, :, columns]], axis=1)
+        r = tn(left, jnp.concatenate([split[0], split[1]], axis=1))
+        return (r[:128, :RANK] + r[128:, RANK:]) + (r[:128, RANK:] + r[128:, :RANK])
+
+    halves = remote(half.at[0], from_core, gcs, gcr, core)
+
+    def both_halves(k):
+        half[k] = gram_half(lax.rem(c + 1 + k, 2))
+
+        @pl.when(k == 0)
+        def _():
+            pl.semaphore_wait(barrier, 1 + (NX * NY - 1) + (NZ - 1))
+            halves.start()
+
+    loop(0, 2, both_halves)
+
+    halves.wait()
+    from_core[...] += half[1]
 
     def rows_of(cx, cy):
         return pl.ds(pl.multiple_of((cx * NY + cy) * 8, 8), 8)
@@ -161,13 +177,13 @@
         remote(from_core.at[rows], from_xy.at[k - 1], gxs, gxr, on_plane(k)).start()
 
     own = rows_of(x, y)
-    loop(1, NX * NY, scatter)
+    plane(scatter)
     remote(from_xy, from_xy, gxs, gxr, core).wait()
     total = from_core[own, :]
     for k in range(NX * NY - 1):
         total += from_xy[k]
     piece[...] = total
-    loop(1, NZ, lambda k: remote(piece, from_z.at[z], gzs, gzr, along_z(k)).start())
+    ring(lambda k: remote(piece, from_z.at[z], gzs, gzr, along_z(k)).start())
     from_z[z] = total
     remote(from_z.at[pl.ds(0, NZ - 1)], from_z.at[pl.ds(0, NZ - 1)], gzs, gzr, core).wait()
     total = from_z[0]
@@ -177,10 +193,10 @@
     mine_of_gram = gram.at[c, own]
 
     def back(k):
-        return remote(mine_of_gram, mine_of_gram, gbs, gbr.at[k - 1], on_plane(k))
-
-    loop(1, NX * NY, lambda k: back(k).start())
-    loop(1, NX * NY, lambda k: back(k).wait_recv())
+        return remote(mine_of_gram, mine_of_gram, gbs, gbr, on_plane(k))
+
+    plane(lambda k: back(k).start())
+    remote(from_xy, from_xy, gbs, gbr, core).wait_recv()
     copy = remote(gram.at[c], gram.at[c], ghs, ghr, core)
     copy.start()
     copy.wait()
@@ -193,9 +209,13 @@
         lax.broadcasted_iota(jnp.int32, (RANK, RANK), 0)
         == lax.broadcasted_iota(jnp.int32, (RANK, RANK), 1)
     ).astype(f32)
+    d = work[:n, :n]
     for b in range(RANK // n):
         lo, hi = b * n, (b + 1) * n
-        inv = factor_block(work[lo:hi, lo:hi])
+        inv = factor_block(d)
+        if hi < RANK:
+            near = nt(work[hi : hi + n, lo:hi], inv, HIGHEST)
+            d = work[hi : hi + n, hi : hi + n] - nt(near, near, HIGHEST)
         r = jnp.dot(inv, work[lo:hi, :], precision=HIGHEST, preferred_element_type=f32)
         inverse[lo:hi, :] = r[:, RANK:]
         if hi < RANK:
@@ -250,9 +270,13 @@
                     rows = pl.ds(pl.multiple_of(RAB + lax.rem(z + k, NZ) * 8, 8), 8)
                     remote(sums.at[group, rows], c1.at[k - 1, group], c1s, c1r, along_z(k)).start()
 
-                loop(1, NZ, to_z)
-
-    loop(0, blocks + lag, step)
+                ring(to_z)
+
+    def steps(g):
+        for q in range(4):
+            step(g * 4 + q)
+
+    loop(0, (blocks + lag) // 4, steps)
 
     def a_sum(j):
         remote(a1.at[j], a1.at[j], a1s, a1r.at[j], core).wait_recv()
@@ -280,7 +304,7 @@
         rows = pl.ds(pl.multiple_of(lax.rem(z + k, NZ) * share, 8), share)
         remote(mine.at[rows], z1.at[k - 1], zs, zr, along_z(k)).start()
 
-    loop(1, NZ, to_z1)
+    ring(to_z1)
 
     remote(c1, c1, c1s, c1r, core).wait_recv()
     own_rows = pl.ds(pl.multiple_of(RAB + z * 8, 8), 8)
@@ -294,11 +318,11 @@
         j = lax.rem(lax.rem(k, NY) + NY - 1, NY)
         remote(csum.at[i * NY + j], c2.at[k - 1], c2s, c2r, on_plane(k)).start()
 
-    loop(1, blocks, to_plane)
+    plane(to_plane)
 
     def gather(rows, which):
         def one(k):
-            return remote(out_ref.at[rows], out_ref.at[rows], ws.at[which], wr.at[which, k - 1], along_z(k))
+            return remote(out_ref.at[rows], out_ref.at[rows], ws.at[which], wr.at[which], along_z(k))
 
         return one
 
@@ -309,14 +333,14 @@
         total += z1[k]
     out_ref[rows, :] = total
     large = gather(rows, 0)
-    loop(1, NZ, lambda k: large(k).start())
+    ring(lambda k: large(k).start())
     total = csum[blocks - 1]
     remote(c2, c2, c2s, c2r, core).wait()
     for k in range(blocks - 1):
         total += c2[k]
     out_ref[own_rows, :] = total
     small = gather(own_rows, 1)
-    loop(1, NZ, lambda k: small(k).start())
+    ring(lambda k: small(k).start())
     remote(z1, z1, ws.at[0], zr, core).wait_send()
     remote(c2.at[pl.ds(0, NZ - 1)], c2.at[pl.ds(0, NZ - 1)], ws.at[1], zr, core).wait_send()
     remote(term.at[1], sums, cs, zr, core).wait_send()
@@ -326,8 +350,8 @@
     remote(a2.at[0], a2.at[1], a2s, zr, core).wait_send()
     remote(b2.at[0], b2.at[1], b2s, zr, core).wait_send()
     out_copy.wait()
-    loop(1, NZ, lambda k: large(k).wait_recv())
-    loop(1, NZ, lambda k: small(k).wait_recv())
+    remote(z1, z1, zs, wr.at[0], core).wait_recv()
+    remote(c2.at[pl.ds(0, NZ - 1)], c2.at[pl.ds(0, NZ - 1)], zs, wr.at[1], core).wait_recv()
 
 
 def sems(*shape):
@@ -353,6 +377,7 @@
             pltpu.VMEM((ROWS, SNAPS), bf16),
             pltpu.VMEM((SNAPS, RANK), bf16),
             pltpu.VMEM((ROWS, RANK), f32),
+            pltpu.VMEM((2, ROWS, RANK), bf16),
             pltpu.VMEM((ROWS, RANK), f32),
             pltpu.VMEM((2, 128, RANK), f32),
             pltpu.VMEM((128, RANK), f32),
@@ -375,11 +400,11 @@
             pltpu.VMEM((RAB, 128), f32),
             pltpu.VMEM((7, RAB // NZ, 128), f32),
             sems(PARTS + 1), sems(),
-            sems(), sems(), sems(), sems(), sems(), sems(), sems(), sems(15), sems(), sems(),
+            sems(), sems(), sems(), sems(), sems(), sems(), sems(), sems(), sems(), sems(),
             sems(), sems(16),
             sems(), sems(NY), sems(), sems(NX), sems(), sems(),
             sems(), sems(), sems(), sems(), sems(), sems(),
-            sems(), sems(), sems(2), sems(2, 7),
+            sems(), sems(), sems(2), sems(2),
         ],
         compiler_params=pltpu.CompilerParams(
             collective_id=0, has_side_effects=True, vmem_limit_bytes=56 * 2**20

time: 70.5 us -> 68.1 us (0.966)
  Pallas kernels: 68.8 us -> 66.9 us
    pallas_call x1, Pallas kernels: 66.5 us -> 64.6 us  [local(): pl.pallas_call(kernel, name='range_finder', out_shape=(jax.ShapeDtypeStru...]
where the time goes in v4:
time: 68.1 us; the launch traced here: 67.5 us
  Pallas kernels  66.9 us (98%)
    pallas_call x1, Pallas kernels, local(): pl.pallas_call(kernel, name='range_finder', out_shape=(jax.ShapeDtypeStru...  64.6 us
    pallas_call x1, Pallas kernels, local(): pl.pallas_call(finish, name='finish', out_shape=(jax.ShapeDtypeStruct((RO...  2.31 us

profile of v4, /device:TPU:32, one launch (start us, length us, event | category | flops | bytes accessed | tf_op | source)
XLA Modules:
  0.0 67.5 jit_solution(6625073870073058939)
XLA Ops:
  0.6 64.6 %range_finder.1 = (f32[1024,256]{1,0:T(8,128)}, f32[256,128]{1,0:T(8,128)}) custom-call(bf16[1024,4096]{1,0:T(8,128)(2,1)} %snap_ref.1, bf16[4096,256]{1,0:T(8,128)(2,1)} %test_ref.1), custom_call_target="tpu_custom_call" | custom-call | tf_op jit(solution)/shard_map/range_finder/pallas_call | solution.py:367
  65.2 2.3 %finish.1 = (f32[1024,256]{1,0:T(8,128)}, f32[128,256]{1,0:T(8,128)}) custom-call(f32[1024,256]{1,0:T(8,128)} %get-tuple-element.4.basis_in, f32[256,128]{1,0:T(8,128)} %get-tuple-element.5.flat), custom_call_target="tpu_custom_call" | custom-call | tf_op jit(solution)/shard_map/finish/pallas_call | solution.py:413

commit v5 on v4

--- a/solution.py
+++ b/solution.py
@@ -166,6 +166,10 @@
 
     loop(0, 2, both_halves)
 
+    work[:, RANK:] = (
+        lax.broadcasted_iota(jnp.int32, (RANK, RANK), 0)
+        == lax.broadcasted_iota(jnp.int32, (RANK, RANK), 1)
+    ).astype(f32)
     halves.wait()
     from_core[...] += half[1]
 
@@ -205,10 +209,6 @@
     n = 64
     work[:128, :RANK] = gram[0]
     work[128:, :RANK] = gram[1]
-    work[:, RANK:] = (
-        lax.broadcasted_iota(jnp.int32, (RANK, RANK), 0)
-        == lax.broadcasted_iota(jnp.int32, (RANK, RANK), 1)
-    ).astype(f32)
     d = work[:n, :n]
     for b in range(RANK // n):
         lo, hi = b * n, (b + 1) * n
@@ -230,6 +230,10 @@
     out_copy = pltpu.make_async_copy(basis, basis_ref, store)
     out_copy.start()
 
+    def off(i):
+        h, r = lax.div(i, 2), lax.rem(i, 2)
+        return 2 - r + h * (1 + 2 * r)
+
     to_a, to_b = pl.ds(0, RA), pl.ds(RA, RB)
     blocks = NX * NY
     lag = 4
@@ -240,7 +244,7 @@
     def step(n):
         @pl.when(n < blocks)
         def _():
-            cx, cy = lax.rem(x + 1 + lax.div(n, NY), NX), lax.rem(y + 1 + lax.rem(n, NY), NY)
+            cx, cy = lax.rem(x + off(lax.div(n, NY)), NX), lax.rem(y + off(lax.rem(n, NY)), NY)
             columns = pl.ds(pl.multiple_of((cx * NY + cy) * 256, 256), 256)
             r = jnp.dot(flipped[...], snap[:, columns], preferred_element_type=f32)
             term[c, n] = r[:, :128]
@@ -256,11 +260,11 @@
 
             @pl.when(i < NX - 1)
             def _():
-                remote(sums.at[m, to_a], a1.at[j, i], a1s, a1r.at[j], along_x(i + 1)).start()
+                remote(sums.at[m, to_a], a1.at[j, i], a1s, a1r.at[j], along_x(off(i))).start()
 
             @pl.when(j < NY - 1)
             def _():
-                remote(sums.at[m, to_b], b1.at[i, j], b1s, b1r.at[i], along_y(j + 1)).start()
+                remote(sums.at[m, to_b], b1.at[i, j], b1s, b1r.at[i], along_y(off(j))).start()
 
             @pl.when(j == NY - 1)
             def _():
@@ -286,12 +290,13 @@
         remote(b1.at[i], b1.at[i], b1s, b1r.at[i], core).wait_recv()
         return sums[i * NY + NY - 1, RA:RAB] + (b1[i, 0] + b1[i, 1] + b1[i, 2])
 
+    near = (2, 1, 3)
     for k in range(3):
         b2[0, k] = b_sum(k)
-        remote(b2.at[0, k], b2.at[1, k], b2s, b2r, along_x(k + 1)).start()
+        remote(b2.at[0, k], b2.at[1, k], b2s, b2r, along_x(near[k])).start()
     for k in range(3):
         a2[0, k] = a_sum(k)
-        remote(a2.at[0, k], a2.at[1, k], a2s, a2r, along_y(k + 1)).start()
+        remote(a2.at[0, k], a2.at[1, k], a2s, a2r, along_y(near[k])).start()
     mine[RA:] = b_sum(3)
     mine[:RA] = a_sum(3)
     remote(a2.at[0], a2.at[1], a2s, a2r, core).wait_recv()
@@ -313,10 +318,12 @@
         total += c1[k]
     csum[...] = total
 
+    def block_at(d):
+        h, r = lax.div(d, 2), lax.rem(d, 2)
+        return 3 - 2 * r - 3 * h + 4 * h * r
+
     def to_plane(k):
-        i = lax.rem(lax.div(k, NY) + NX - 1, NX)
-        j = lax.rem(lax.rem(k, NY) + NY - 1, NY)
-        remote(csum.at[i * NY + j], c2.at[k - 1], c2s, c2r, on_plane(k)).start()
+        remote(csum.at[block_at(lax.div(k, NY)) * NY + block_at(lax.rem(k, NY))], c2.at[k - 1], c2s, c2r, on_plane(k)).start()
 
     plane(to_plane)
 

time: 68.1 us -> 67.7 us (level)
  no operation moved by 1% of the time
where the time goes in v5:
time: 67.7 us; the launch traced here: 67.5 us
  Pallas kernels  66.9 us (99%)
    pallas_call x1, Pallas kernels, local(): pl.pallas_call(kernel, name='range_finder', out_shape=(jax.ShapeDtypeStru...  64.6 us
    pallas_call x1, Pallas kernels, local(): pl.pallas_call(finish, name='finish', out_shape=(jax.ShapeDtypeStruct((RO...  2.31 us

profile of v5, /device:TPU:32, one launch (start us, length us, event | category | flops | bytes accessed | tf_op | source)
XLA Modules:
  0.0 67.5 jit_solution(11340625131419648532)
XLA Ops:
  0.6 64.6 %range_finder.1 = (f32[1024,256]{1,0:T(8,128)}, f32[256,128]{1,0:T(8,128)}) custom-call(bf16[1024,4096]{1,0:T(8,128)(2,1)} %snap_ref.1, bf16[4096,256]{1,0:T(8,128)(2,1)} %test_ref.1), custom_call_target="tpu_custom_call" | custom-call | tf_op jit(solution)/shard_map/range_finder/pallas_call | solution.py:374
  65.2 2.3 %finish.1 = (f32[1024,256]{1,0:T(8,128)}, f32[128,256]{1,0:T(8,128)}) custom-call(f32[1024,256]{1,0:T(8,128)} %get-tuple-element.4.basis_in, f32[256,128]{1,0:T(8,128)} %get-tuple-element.5.flat), custom_call_target="tpu_custom_call" | custom-call | tf_op jit(solution)/shard_map/finish/pallas_call | solution.py:420

commit v6 on v5

--- a/solution.py
+++ b/solution.py
@@ -291,14 +291,23 @@
         return sums[i * NY + NY - 1, RA:RAB] + (b1[i, 0] + b1[i, 1] + b1[i, 2])
 
     near = (2, 1, 3)
-    for k in range(3):
+
+    def second_a(k):
+        a2[0, k] = a_sum(k)
+        remote(a2.at[0, k], a2.at[1, k], a2s, a2r, along_y(near[k])).start()
+
+    def second_b(k):
         b2[0, k] = b_sum(k)
         remote(b2.at[0, k], b2.at[1, k], b2s, b2r, along_x(near[k])).start()
-    for k in range(3):
-        a2[0, k] = a_sum(k)
-        remote(a2.at[0, k], a2.at[1, k], a2s, a2r, along_y(near[k])).start()
+
+    second_b(0)
+    second_b(1)
+    second_a(0)
+    second_a(1)
+    second_b(2)
+    second_a(2)
+    mine[:RA] = a_sum(3)
     mine[RA:] = b_sum(3)
-    mine[:RA] = a_sum(3)
     remote(a2.at[0], a2.at[1], a2s, a2r, core).wait_recv()
     remote(b2.at[0], b2.at[1], b2s, b2r, core).wait_recv()
     mine[:RA] += a2[1, 0] + a2[1, 1] + a2[1, 2]

time: 67.7 us -> 67.7 us (level)
  no operation moved by 1% of the time
where the time goes in v6:
time: 67.7 us; the launch traced here: 67.6 us
  Pallas kernels  66.9 us (99%)
    pallas_call x1, Pallas kernels, local(): pl.pallas_call(kernel, name='range_finder', out_shape=(jax.ShapeDtypeStru...  64.6 us
    pallas_call x1, Pallas kernels, local(): pl.pallas_call(finish, name='finish', out_shape=(jax.ShapeDtypeStruct((RO...  2.31 us

profile of v6, /device:TPU:32, one launch (start us, length us, event | category | flops | bytes accessed | tf_op | source)
XLA Modules:
  0.0 67.6 jit_solution(8034466955129689609)
XLA Ops:
  0.6 64.6 %range_finder.1 = (f32[1024,256]{1,0:T(8,128)}, f32[256,128]{1,0:T(8,128)}) custom-call(bf16[1024,4096]{1,0:T(8,128)(2,1)} %snap_ref.1, bf16[4096,256]{1,0:T(8,128)(2,1)} %test_ref.1), custom_call_target="tpu_custom_call" | custom-call | tf_op jit(solution)/shard_map/range_finder/pallas_call | solution.py:383
  65.3 2.3 %finish.1 = (f32[1024,256]{1,0:T(8,128)}, f32[128,256]{1,0:T(8,128)}) custom-call(f32[1024,256]{1,0:T(8,128)} %get-tuple-element.4.basis_in, f32[256,128]{1,0:T(8,128)} %get-tuple-element.5.flat), custom_call_target="tpu_custom_call" | custom-call | tf_op jit(solution)/shard_map/finish/pallas_call | solution.py:429
